TPU v7x, 128 devices: a whole 4x4x4 slice. The times are simulated.
128 devices in a mesh: row: 8 (over x, core), col: 16 (over z, y).
Axes of the slice: x: 4, y: 4, z: 4, core: 2. Of those that a mesh axis runs over, the one named last changes fastest.
Arguments:
- bem: float32 [2, 16384, 16384], P(None, 'row', 'col'), may hold values from -0.0625 to 0.0625
- face_disp: float32 [2, 25, 512, 2048], P(None, None, 'col', 'row'), may hold values from -6 to 6
- face_map: float32 [16, 25, 2048], P(None, None, 'row'), may hold values from -1.25 to 1.25
- dof_count: int32 [2048], P('row'), may hold values from 9 to 25, as said below
- elem_target: int32 [2048], replicated, may hold values from 0 to 1023, as said below
- live_count: int32 [8], replicated, may hold values from 0 to 256, as said below
- forward_field: float32 [2, 512, 16384], P(None, None, ('col', 'row')), may hold values from -6 to 6
- power_weight: float32 [512], replicated, may hold values from 0.02 to 0.2
Outputs:
- adjoint_field: float32 [2, 512, 16384], P(None, None, ('col', 'row'))
- gradient: float32 [16384], P(('col', 'row'))
Inputs may be any that keep to these rules, and one draw needn't show every extreme that they name: `dof_count`: face nodes of an element of order 2, 3 or 4: 9, 16 or 25. `live_count`: every owner's count is a multiple of 8, the counts sum to 1024, and one owner holds 256. `elem_target`: the live slots name every position 0 to 1023 exactly once; block b = position // 128. The live slots of one owner name each block equally often, at most 32 times, and one owner names every block exactly 32 times. Slots that are not live hold 0.
All inputs are finite; a program needn't handle non-finite values.
Results may differ from a plain program's by a relative error of at most 0.000092.
Values sent between devices are 32-bit elements; how exact they have to be, the bound alone decides.
A program may use at most 320 MiB of HBM per device.

v0:
```python
import jax
import jax.numpy as jnp
from jax import lax
from jax.sharding import PartitionSpec as P

PTS = 16


HIGHEST = lax.Precision.HIGHEST


def surface_traction(face_map, face_disp, dof_count):
    nodes = face_map.shape[1]
    active = lax.broadcasted_iota(jnp.int32, (nodes, dof_count.shape[0]), 0) < dof_count[None, :]
    masked = face_map * active.astype(face_map.dtype)[None]
    return jnp.einsum("pqe,lqre->lpre", masked, face_disp, precision=HIGHEST)


def on_device(
    bem, face_disp, face_map, dof_count, elem_target, live_count, forward_field, power_weight
):
    owners = live_count.shape[0]
    elem_cap = elem_target.shape[0] // owners
    per_block = bem.shape[1] // PTS
    my_block = lax.axis_index("row")
    targets = elem_target.reshape(owners, elem_cap)
    slot_idx = lax.broadcasted_iota(jnp.int32, (owners, elem_cap), 1)
    living = slot_idx < live_count[:, None]
    blocks = targets // per_block
    within = targets % per_block
    traction = surface_traction(face_map, face_disp, dof_count)
    for_me_flat = (living & (blocks == my_block)).reshape(-1)
    column_ids = lax.broadcasted_iota(jnp.int32, (owners * elem_cap, per_block), 1)
    placer_all = (for_me_flat[:, None] & (within.reshape(-1)[:, None] == column_ids)).astype(
        jnp.float32
    )
    adjoint_part = jnp.einsum(
        "lprs,sw->lprw",
        lax.all_gather(traction, "row", axis=3, tiled=True),
        placer_all,
        precision=HIGHEST,
    )
    blocked = bem.reshape(2, PTS, per_block, bem.shape[2])
    products = jnp.einsum(
        "lprw,apwk->lark",
        lax.all_gather(adjoint_part, "col", axis=2, tiled=True),
        blocked,
        precision=HIGHEST,
    )
    partial_value = jnp.stack([products[0, 0] - products[1, 1], products[1, 0] + products[0, 1]])
    adjoint_field = lax.psum_scatter(partial_value, "row", scatter_dimension=2, tiled=True)
    gradient = jnp.sum(
        power_weight[:, None]
        * (forward_field[0] * adjoint_field[0] + forward_field[1] * adjoint_field[1]),
        axis=0,
    )
    return (adjoint_field, gradient)


def solution(mesh):
    placed = (
        P(None, "row", "col"),
        P(None, None, "col", "row"),
        P(None, None, "row"),
        P("row"),
        P(),
        P(),
        P(None, None, ("col", "row")),
        P(),
    )
    return jax.shard_map(
        on_device,
        mesh=mesh,
        in_specs=placed,
        out_specs=(P(None, None, ("col", "row")), P(("col", "row"))),
        check_vma=False,
    )
```

profile of v0, /device:TPU:1, one launch (start us, length us, event | category | flops | bytes accessed | tf_op | source)
XLA Modules:
  0.0 269.9 jit_solution(16211334729418468787)
XLA Ops:
  7.2 0.0 all-gather.3.cloned.1.call-start
  7.2 0.7 fusion.17
  7.9 1.0 multiply_bitcast_fusion
  8.9 1.4 copy.10
  10.3 8.4 %copy.11 = f32[2,25,32,256]{2,1,0,3:T(8,128)} copy(f32[2,25,32,256]{3,2,1,0:T(8,128)} %param.9) | data formatting | bytes 3276800 | tf_op args[1]
  18.7 8.2 %fusion.22 = f32[256,16,2,32]{3,1,2,0:T(8,128)} fusion(f32[16,25,256,1]{1,0,3,2:T(8,128)S(1)} %copy.10, f32[2,25,32,256]{2,1,0,3:T(8,128)} %copy.11), kind=kOutput, calls=%fused_computation.34 | convolution fusion | flops 78643200 | bytes 3096576 | tf_op jit(solution)/shard_map/pqe,lqre->lpre/dot_general | solution.py:16
  26.8 0.0 copy-start.3
  26.8 0.0 copy-start.1
  26.8 4.4 %copy.12 = f32[256,16,2,32]{0,3,1,2:T(8,128)} copy(f32[256,16,2,32]{3,1,2,0:T(8,128)} %fusion.22) | data formatting | bytes 2097152 | tf_op jit(solution)/shard_map/pqe,lqre->lpre/dot_general | solution.py:16
  31.2 0.0 all-gather.3.cloned.1.call-update
  31.3 0.0 all-gather.5.cloned.1.call-start
  31.3 0.0 copy-done.3
  31.3 0.1 iota_compare_fusion.2
  31.4 0.0 copy-done.1
  31.5 53.2 %all-gather.3.cloned.1.call-done = f32[2,16,32,2048]{3,2,1,0:T(8,128)} async-done(((f32[2,16,32,256]{3,2,1,0:T(8,128)}), f32[2,16,32,2048]{3,2,1,0:T(8,128)}) %all-gather.3.cloned.1.call-update) | async-done | bytes 8388624 | tf_op jit(solution)/shard_map/all_gather | solution.py:39
  84.7 8.2 %fusion.9 = f32[2,16,32,128]{3,2,1,0:T(8,128)} fusion(f32[2,16,32,2048]{3,2,1,0:T(8,128)} %all-gather.3.cloned.1.call-done, s32[2048]{0:T(1024)S(1)} %add_select_fusion, pred[2048]{0:T(1024)(128)(4,1)S(1)} %fusion.20), kind=kOutput, calls=%fused_computation.11 | convolution fusion | flops 3221749760 | bytes 8923136 | tf_op jit(solution)/shard_map/lprs,sw->lprw/dot_general | solution.py:37
  92.9 0.0 all-gather.5.cloned.1.call-update
  92.9 0.0 reduce-scatter.2.cloned.1.call-start
  93.0 70.8 %all-gather.5.cloned.1.call-done = f32[2,16,512,128]{3,2,1,0:T(8,128)} async-done(((f32[2,16,32,128]{3,2,1,0:T(8,128)}), f32[2,16,512,128]{3,2,1,0:T(8,128)}) %all-gather.5.cloned.1.call-update) | async-done | bytes 8388624 | tf_op jit(solution)/shard_map/all_gather | solution.py:46
  163.8 60.1 %fusion.2 = f32[2,2,512,1024]{3,2,1,0:T(8,128)S(1)} fusion(f32[2,16,128,1024,1]{3,2,1,0,4:T(8,128)} %bitcast.38, f32[2,16,512,128]{3,2,1,0:T(8,128)} %all-gather.5.cloned.1.call-done), kind=kOutput, calls=%fused_computation.3 | convolution fusion | flops 51539607552 | bytes 33554432 | tf_op jit(solution)/shard_map/lprw,apwk->lark/dot_general | solution.py:44
  223.9 0.9 fusion.6
  224.8 2.2 pad_maximum_fusion
  227.1 0.0 copy-start
  227.1 0.0 copy-start.2
  227.1 0.0 reduce-scatter.2.cloned.1.call-update
  227.1 34.6 %reduce-scatter.2.cloned.1.call-done = f32[2,512,128]{2,1,0:T(8,128)} async-done(((f32[2,512,1024]{2,1,0:T(8,128)}), f32[2,512,128]{2,1,0:T(8,128)}) %reduce-scatter.2.cloned.1.call-update) | async-done | bytes 524304 | tf_op jit(solution)/shard_map/reduce_scatter | solution.py:51
  261.7 0.0 copy-done
  261.7 0.0 copy-done.2
  261.7 1.7 fusion.16
  (3 shorter events, 0.0 us)
Async XLA Ops:
  7.2 77.5 %all-gather.3.cloned.1.call-start = ((), (), s32[]{:S(2)}) async-start(), calls=%async_computation.1 | async-start | bytes 9437184 | tf_op jit(solution)/shard_map/all_gather | solution.py:39
  26.8 4.5 %copy-start.3 = (s32[8]{0:T(128)S(1)}, s32[8]{0:T(128)}, u32[]{:S(2)}) copy-start(s32[8]{0:T(128)} %param.13) | copy-start | bytes 100
  26.8 4.6 %copy-start.1 = (s32[2048]{0:T(1024)S(1)}, s32[2048]{0:T(1024)}, u32[]{:S(2)}) copy-start(s32[2048]{0:T(1024)} %param.12) | copy-start | bytes 24580
  31.3 132.5 %all-gather.5.cloned.1.call-start = ((), (), s32[]{:S(2)}) async-start(), calls=%async_computation.2 | async-start | bytes 8912896 | tf_op jit(solution)/shard_map/all_gather | solution.py:46
  92.9 168.8 %reduce-scatter.2.cloned.1.call-start = ((), (), s32[]{:S(2)}) async-start(), calls=%async_computation.3 | async-start | bytes 4718592 | tf_op jit(solution)/shard_map/reduce_scatter | solution.py:51
  227.1 34.6 %copy-start = (f32[2,512,128]{2,1,0:T(8,128)S(1)}, f32[2,512,128]{2,1,0:T(8,128)}, u32[]{:S(2)}) copy-start(f32[2,512,128]{2,1,0:T(8,128)} %param.14) | copy-start | bytes 1572868
  227.1 34.6 %copy-start.2 = (f32[512]{0:T(512)S(1)}, f32[512]{0:T(512)}, u32[]{:S(2)}) copy-start(f32[512]{0:T(512)} %param.15) | copy-start | bytes 6148
Sparse Core Ops, SparseCore 0:
  31.4 53.2 all-gather.2
  93.0 70.6 all-gather.4
  227.2 34.4 reduce-scatter.1
where the time goes:
time: 272 us; the launch traced here: 270 us
  waiting for transfers between devices  159 us (58%)
  matrix products  76.5 us (28%)
  local copies, waits for them, and re-layouts  14.1 us (5%)
  between operations  13.8 us (5%)
  other arithmetic  6.69 us (2%)
    all_gather x1, waiting for transfers between devices, on_device(): lax.all_gather(adjoint_part, 'col', axis=2, tiled=True)  70.8 us
    dot_general x1, matrix products, on_device(): jnp.einsum('lprw,apwk->lark', lax.all_gather(adjoint_part, 'col', axis=2,...  60.1 us
    all_gather x1, waiting for transfers between devices, on_device(): lax.all_gather(traction, 'row', axis=3, tiled=True)  53.2 us
    reduce_scatter x1, waiting for transfers between devices, on_device(): lax.psum_scatter(partial_value, 'row', scatter_dimension=2, tiled=True)  34.6 us
    unnamed x9, local copies, waits for them, and re-layouts  8.37 us
    dot_general x1, matrix products, on_device(): jnp.einsum('lprs,sw->lprw', lax.all_gather(traction, 'row', axis=3, tiled...  8.21 us
    dot_general x1, matrix products, surface_traction(): return jnp.einsum('pqe,lqre->lpre', masked, face_disp, precision=HIGHEST)  8.17 us
  transfers between devices with their start and end apart: 3, of which 3 were waited for; matrix products, arithmetic and copies ran while one was open for 0% of the time, Pallas kernels for 0%

commit v1 on v0

v1 whole, which is shorter than its diff:
```python
import functools

import jax
import jax.numpy as jnp
from jax import lax
from jax.experimental import pallas as pl
from jax.experimental.pallas import tpu as pltpu
from jax.sharding import PartitionSpec as P

MESH = pl.DeviceIdType.MESH
F32 = jnp.float32
BF16 = jnp.bfloat16

CHUNKS = 4
START = 8
LAST = START + 4 * CHUNKS
STAGES = {
    3: [(1, 0)],
    4: [(1, 1)],
    5: [(2, 0)],
    6: [(2, 1), (1, 2)],
    7: [(3, 0)],
    9: [(3, 1), (1, 3)],
    10: [(2, 2)],
    11: [(2, 3)],
    13: [(3, 2)],
    15: [(3, 3)],
}


def nt(a, b):
    return lax.dot_general(a, b, (((1,), (1,)), ((), ())), preferred_element_type=F32)


def nn(a, b):
    return jnp.dot(a, b, preferred_element_type=F32)


def halves(value):
    high = value.astype(BF16)
    return high, (value - high.astype(F32)).astype(BF16)


def one_hot(condition):
    return jnp.where(condition, 1.0, 0.0).astype(BF16)


def kernel(
    live_ref, target_ref, dof_ref, weight_ref, bem_ref, disp_ref, map_ref, fwd_ref,
    field_ref, grad_ref,
    disp, fmap, fwd, stage, pick, spread, trac, comp, got, rhs, rhs_hi, rhs_lo, bem_hi, bem_lo,
    mine, theirs, joined, partial, grad,
    in_sem, bem_sem, swap_s, swap_r, ag_s, ag_r, pair_s, pair_r, sum_s, sum_r,
):
    row = lax.axis_index("row")
    col = lax.axis_index("col")
    x, core = row // 2, row % 2
    z, y = col // 4, col % 4

    barrier = pltpu.get_barrier_semaphore()
    for d in range(1, 8):
        pl.semaphore_signal(barrier, inc=1, device_id=((row + d) % 8, col), device_id_type=MESH)
    for d in (1, 3):
        near = ((z + d) % 4) * 4 + y
        pl.semaphore_signal(barrier, inc=1, device_id=(row, near), device_id_type=MESH)
        near = z * 4 + (y + d) % 4
        pl.semaphore_signal(barrier, inc=1, device_id=(row, near), device_id_type=MESH)

    loads = [
        pltpu.make_async_copy(map_ref, fmap, in_sem.at[0]),
        pltpu.make_async_copy(disp_ref, disp, in_sem.at[1]),
        pltpu.make_async_copy(fwd_ref, fwd, in_sem.at[2]),
    ]

    def bem_load(i):
        rows = pl.ds(pl.multiple_of(i * 256, 256), 256)
        return pltpu.make_async_copy(
            bem_ref.at[:, rows, :], stage.at[i % 2], bem_sem.at[i % 2]
        )

    loads[0].start()
    loads[1].start()
    bem_load(0).start()
    bem_load(1).start()
    loads[2].start()

    lane = lax.broadcasted_iota(jnp.int32, (8, 256), 1)
    line = lax.broadcasted_iota(jnp.int32, (8, 256), 0)
    count = jnp.zeros((8, 256), jnp.int32)
    for o in range(8):
        count = jnp.where(line == o, live_ref[o], count)
    live = lane < count
    target = target_ref[...]
    block = target >> 7
    within = target & 127
    members = jnp.concatenate(
        [jnp.where(live & (block == b), 1.0, 0.0) for b in range(8)], axis=0
    )
    before = lax.broadcasted_iota(jnp.int32, (256, 256), 0) < lax.broadcasted_iota(
        jnp.int32, (256, 256), 1
    )
    ranks = members * nn(members.astype(BF16), one_hot(before))
    rank = ranks[0:8]
    for b in range(1, 8):
        rank = rank + ranks[b * 8 : b * 8 + 8]
    place = jnp.where(live, block * 32 + rank.astype(jnp.int32), -1)
    own = jnp.sum(jnp.where(line == row, place, 0), axis=0, keepdims=True)
    tall = lax.broadcasted_iota(jnp.int32, (256, 256), 0)
    pick[...] = one_hot(tall == own)
    wide = lax.broadcasted_iota(jnp.int32, (128, 256), 0)
    here = jnp.where(live & (block == row), place - row * 32 + line * 32, -1)
    total = jnp.zeros((128, 256), F32)
    for o in range(8):
        total = total + nt(
            one_hot(wide == within[o : o + 1]), one_hot(tall == here[o : o + 1])
        )
    spread[...] = total.astype(BF16)
    grad[...] = jnp.zeros_like(grad)

    loads[0].wait()
    node = lax.broadcasted_iota(jnp.int32, (25, 256), 0)
    used = node < dof_ref[...]
    for p in range(16):
        fmap[p] = jnp.where(used, fmap[p], 0.0)
    loads[1].wait()

    pl.semaphore_wait(barrier, 11)

    def swap(j, d):
        to = (row + d) % 8
        return pltpu.make_async_remote_copy(
            comp.at[j, pl.ds(pl.multiple_of(to * 32, 32), 32), :],
            got.at[j, pl.ds(pl.multiple_of(row * 32, 32), 32), :],
            swap_s.at[j, d - 1], swap_r.at[j, d - 1],
            device_id=(to, col), device_id_type=MESH,
        )

    def swap_in(j, d):
        origin = (row + 8 - d) % 8
        return pltpu.make_async_remote_copy(
            comp.at[j, pl.ds(pl.multiple_of(row * 32, 32), 32), :],
            got.at[j, pl.ds(pl.multiple_of(origin * 32, 32), 32), :],
            swap_s.at[j, d - 1], swap_r.at[j, d - 1],
            device_id=((row + d) % 8, col), device_id_type=MESH,
        )

    def tractions(j):
        eight = pl.ds(pl.multiple_of(j * 8, 8), 8)
        for group in range(4):
            sums = [[None] * 4, [None] * 4]
            for q in range(25):
                value = [disp[l, q, eight, :] for l in range(2)]
                for k in range(4):
                    scale = fmap[group * 4 + k, q : q + 1, :]
                    for l in range(2):
                        term = scale * value[l]
                        sums[l][k] = term if q == 0 else sums[l][k] + term
            for l in range(2):
                for k in range(4):
                    at = l * 128 + (group * 4 + k) * 8
                    trac[at : at + 8, :] = sums[l][k]
        high, low = halves(trac[...])
        comp[j] = nt(pick[...], high) + nt(pick[...], low)
        for d in range(1, 8):
            swap(j, d).start()
        rows = pl.ds(pl.multiple_of(row * 32, 32), 32)
        got[j, rows, :] = comp[j, rows, :]

    def slots(f, first, second):
        def sel(v):
            kind, a = v
            return (a // 2, a % 2) if kind == "one" else (slice(None), a)

        fi, se = sel(first), sel(second)
        return fi + se if f == 0 else se + fi

    def part(ref, j, f, first, second, half):
        lanes = slice(None) if half is None else pl.ds(half * 1024, 1024)
        return ref.at[(j,) + slots(f, first, second) + (f, slice(None), lanes)]

    def ring(f):
        return (z, y) if f == 0 else (y, z)

    def away(f, axis, step):
        v1, v2 = ring(f)
        if axis == 0:
            v1 = (v1 + step + 4) % 4
        else:
            v2 = (v2 + step + 4) % 4
        return (row, v1 * 4 + v2) if f == 0 else (row, v2 * 4 + v1)

    def hop(j, f, kind):
        v1, v2 = ring(f)
        step = 1 if kind % 2 == 0 else -1
        back = lambda v, n: (v + 4 - n * step) % 4
        one = lambda v: ("one", v)
        par = ("par", (v1 + 1) % 2)
        far = one((v1 + 2) % 4)
        half = kind % 2
        table = {
            0: (0, (one(v1), one(v2), None), (one(back(v1, 1)), one(v2), None)),
            1: (1, (one(v1), one(v2), None), (one(v1), one(back(v2, 1)), None)),
            2: (0, (one(back(v1, 1)), one(v2), half), (far, one(v2), half)),
            3: (1, (par, one(v2), None), (par, one(back(v2, 1)), None)),
            4: (1, (one(v1), one(back(v2, 1)), half), (one(v1), one((v2 + 2) % 4), half)),
            5: (1, (far, one(v2), None), (far, one(back(v2, 1)), None)),
            6: (1, (par, one(back(v2, 1)), half), (par, one((v2 + 2) % 4), half)),
            7: (1, (far, one(back(v2, 1)), half), (far, one((v2 + 2) % 4), half)),
        }
        axis, out, into = table[kind // 2]
        make = lambda src, dst: pltpu.make_async_remote_copy(
            part(rhs, j, f, *src), part(rhs, j, f, *dst),
            ag_s.at[j, f, kind], ag_r.at[j, f, kind],
            device_id=away(f, axis, step), device_id_type=MESH,
        )
        return lambda: make(out, out), lambda: make(out, into)

    def begin(j, kinds):
        for kind in kinds:
            for f in range(2):
                for s in range(2):
                    hop(j, f, 2 * kind + s)[0]().start()

    def arrive(j, kinds):
        for kind in kinds:
            for f in range(2):
                for s in range(2):
                    hop(j, f, 2 * kind + s)[1]().wait_recv()

    def gather_stage(j, which):
        if which == 1:
            arrive(j, (0,))
            begin(j, (2, 3))
            arrive(j, (1,))
            begin(j, (4,))
        elif which == 2:
            arrive(j, (2,))
            begin(j, (5,))
            arrive(j, (3,))
            begin(j, (6,))
        elif which == 3:
            arrive(j, (5,))
            begin(j, (7,))
        else:
            arrive(j, (4, 6, 7))

    def position(j):
        for d in range(1, 8):
            swap_in(j, d).wait_recv()
        high, low = halves(got[j])
        placed = nn(spread[...], high) + nn(spread[...], low)
        placed = placed.T
        for l in range(2):
            for p in range(16):
                at = l * 128 + p * 8
                rhs[j, z // 2, z % 2, y // 2, y % 2, l, :, p * 128 : p * 128 + 128] = placed[
                    at : at + 8, :
                ]
        begin(j, (0, 1))

    def split_bem(i):
        bem_load(i).wait()

        @pl.loop(0, 16)
        def _(k):
            src = pl.ds(pl.multiple_of(k * 16, 16), 16)
            dst = pl.ds(pl.multiple_of(i * 256 + k * 16, 16), 16)
            for l in range(2):
                high, low = halves(stage[i % 2, l, src, :])
                bem_hi[l, dst, :] = high
                bem_lo[l, dst, :] = low

        @pl.when(i + 2 < 8)
        def _():
            bem_load(i + 2).start()

    def split_rhs(j):
        for c in range(16):
            value = rhs[j, c // 8, (c // 4) % 2, (c // 2) % 2, c % 2].reshape(16, 2048)
            high, low = halves(value)
            rhs_hi[c * 16 : c * 16 + 16, :] = high
            rhs_lo[c * 16 : c * 16 + 16, :] = low

    def pair(j, t):
        return pltpu.make_async_remote_copy(
            theirs.at[j, t], joined.at[j, t], pair_s.at[j, t], pair_r.at[j, t],
            device_id=(x * 2 + 1 - core, col), device_id_type=MESH,
        )

    def share(j, t):
        return pltpu.make_async_remote_copy(
            mine.at[j, t], partial.at[j, t], sum_s.at[j, t], sum_r.at[j, t],
            device_id=(((x + 1 + t) % 4) * 2 + core, col), device_id_type=MESH,
        )

    def multiply(j, t):
        cols = pl.ds(pl.multiple_of(((x + 1 + t) % 4) * 256, 256), 256)
        prod = []
        for l in range(2):
            prod.append(
                (
                    nn(rhs_hi[...], bem_hi[l, :, cols])
                    + nn(rhs_hi[...], bem_lo[l, :, cols])
                    + nn(rhs_lo[...], bem_hi[l, :, cols])
                ).reshape(16, 2, 8, 256)
            )
        both = (prod[0][:, 0] - prod[1][:, 1], prod[0][:, 1] + prod[1][:, 0])
        for l in range(2):
            value = both[l].reshape(128, 256)
            left, right = value[:, :128], value[:, 128:]
            mine[j, t, l] = jnp.where(core == 0, left, right)
            theirs[j, t, l] = jnp.where(core == 0, right, left)
        pair(j, t).start()

    def pass_on(j, t):
        pair(j, t).wait_recv()
        mine[j, t] = mine[j, t] + joined[j, t]

        @pl.when(t < 3)
        def _():
            share(j, t).start()

    def finish(j):
        for t in range(3):
            share(j, t).wait_recv()
        eight = pl.ds(pl.multiple_of(j * 8, 8), 8)
        for l in range(2):
            value = mine[j, 3, l] + partial[j, 0, l] + partial[j, 1, l] + partial[j, 2, l]
            value = value.reshape(16, 8, 128)
            field_ref[l, :, eight, :] = value
            grad[...] += jnp.sum(fwd[l, :, eight, :] * value, axis=0)

    def weigh():
        loads[2].wait()
        weight = jnp.broadcast_to(weight_ref[...], (128, 512)).T.reshape(16, 32, 128)
        for l in range(2):
            fwd[l] = fwd[l] * weight

    @pl.loop(0, LAST)
    def _(s):
        for slot, stages in STAGES.items():
            @pl.when(s == slot)
            def _():
                for which, j in stages:
                    gather_stage(j, which)

        @pl.when(s < CHUNKS)
        def _():
            tractions(s)

        @pl.when((s >= 1) & (s <= CHUNKS))
        def _():
            position(s - 1)

        @pl.when(s < 8)
        def _():
            split_bem(s)

        @pl.when(s == 5)
        def _():
            weigh()

        @pl.when(s >= START)
        def _():
            k = s - START
            j, t = k // 4, k % 4

            @pl.when(t == 0)
            def _():
                gather_stage(j, 4)
                split_rhs(j)

            multiply(j, t)

            @pl.when(k >= 1)
            def _():
                pass_on((k - 1) // 4, (k - 1) % 4)

            @pl.when((t == 2) & (j >= 1))
            def _():
                finish(j - 1)

    pass_on(CHUNKS - 1, 3)
    finish(CHUNKS - 1)
    grad_ref[...] = jnp.sum(grad[...], axis=0, keepdims=True)

    for j in range(CHUNKS):
        for d in range(1, 8):
            swap(j, d).wait_send()
        for f in range(2):
            for kind in range(16):
                hop(j, f, kind)[0]().wait_send()
        for t in range(4):
            pair(j, t).wait_send()
        for t in range(3):
            share(j, t).wait_send()


def on_device(
    bem, face_disp, face_map, dof_count, elem_target, live_count, forward_field, power_weight
):
    vmem = pl.BlockSpec(memory_space=pltpu.VMEM)
    hbm = pl.BlockSpec(memory_space=pl.ANY)
    dma = pltpu.SemaphoreType.DMA
    field, gradient = pl.pallas_call(
        kernel,
        out_shape=(
            jax.ShapeDtypeStruct((2, 16, 32, 128), F32),
            jax.ShapeDtypeStruct((1, 128), F32),
        ),
        in_specs=[pl.BlockSpec(memory_space=pltpu.SMEM), vmem, vmem, vmem, hbm, hbm, hbm, hbm],
        out_specs=(vmem, vmem),
        scratch_shapes=[
            pltpu.VMEM((2, 25, 32, 256), F32),
            pltpu.VMEM((16, 25, 256), F32),
            pltpu.VMEM((2, 16, 32, 128), F32),
            pltpu.VMEM((2, 2, 256, 1024), F32),
            pltpu.VMEM((256, 256), BF16),
            pltpu.VMEM((128, 256), BF16),
            pltpu.VMEM((256, 256), F32),
            pltpu.VMEM((CHUNKS, 256, 256), F32),
            pltpu.VMEM((CHUNKS, 256, 256), F32),
            pltpu.VMEM((CHUNKS, 2, 2, 2, 2, 2, 8, 2048), F32),
            pltpu.VMEM((256, 2048), BF16),
            pltpu.VMEM((256, 2048), BF16),
            pltpu.VMEM((2, 2048, 1024), BF16),
            pltpu.VMEM((2, 2048, 1024), BF16),
            pltpu.VMEM((CHUNKS, 4, 2, 128, 128), F32),
            pltpu.VMEM((CHUNKS, 4, 2, 128, 128), F32),
            pltpu.VMEM((CHUNKS, 4, 2, 128, 128), F32),
            pltpu.VMEM((CHUNKS, 3, 2, 128, 128), F32),
            pltpu.VMEM((8, 128), F32),
            dma((3,)),
            dma((2,)),
            dma((CHUNKS, 7)),
            dma((CHUNKS, 7)),
            dma((CHUNKS, 2, 16)),
            dma((CHUNKS, 2, 16)),
            dma((CHUNKS, 4)),
            dma((CHUNKS, 4)),
            dma((CHUNKS, 3)),
            dma((CHUNKS, 3)),
        ],
        compiler_params=pltpu.CompilerParams(
            collective_id=0, has_side_effects=True, vmem_limit_bytes=60 * 2**20
        ),
        cost_estimate=pl.CostEstimate(
            flops=26 * 10**9, bytes_accessed=20 * 10**6, transcendentals=0
        ),
        name="adjoint",
    )(
        live_count,
        elem_target.reshape(8, 256),
        dof_count.reshape(1, 256),
        power_weight.reshape(1, 512),
        bem,
        face_disp,
        face_map,
        forward_field.reshape(2, 16, 32, 128),
    )
    return field.reshape(2, 512, 128), gradient.reshape(128)


def solution(mesh):
    placed = (
        P(None, "row", "col"),
        P(None, None, "col", "row"),
        P(None, None, "row"),
        P("row"),
        P(),
        P(),
        P(None, None, ("col", "row")),
        P(),
    )
    return jax.shard_map(
        on_device,
        mesh=mesh,
        in_specs=placed,
        out_specs=(P(None, None, ("col", "row")), P(("col", "row"))),
        check_vma=False,
    )
```

time: 272 us -> 99.8 us (0.37)
  waiting for transfers between devices: 159 us -> 0 us
  Pallas kernels: 0 us -> 92 us
  matrix products: 76.5 us -> 0 us
  between operations: 13.8 us -> 0.64 us
  local copies, waits for them, and re-layouts: 14.1 us -> 6.38 us
  other arithmetic: 6.69 us -> 0 us
    all_gather x2 -> x0, waiting for transfers between devices: 124 us -> none  [the longest x1 70.8 us: on_device(): lax.all_gather(adjoint_part, 'col', axis=2, tiled=True)]
    pallas_call x0 -> x1, Pallas kernels: none -> 92 us  [on_device(): pl.pallas_call(kernel, out_shape=(jax.ShapeDtypeStruct((2, 16, 32, 128),...]
    dot_general x3 -> x0, matrix products: 76.5 us -> none  [the longest x1 60.1 us: on_device(): jnp.einsum('lprw,apwk->lark', lax.all_gather(adjoint_part, 'col', axis=2,...]
    reduce_scatter x1 -> x0, waiting for transfers between devices: 34.6 us -> none  [on_device(): lax.psum_scatter(partial_value, 'row', scatter_dimension=2, tiled=True)]
    dot_general x1 -> x0, local copies, waits for them, and re-layouts: 4.39 us -> none  [surface_traction(): return jnp.einsum('pqe,lqre->lpre', masked, face_disp, precision=HIGHEST)]
    unnamed x9 -> x3, local copies, waits for them, and re-layouts: 8.37 us -> 5.09 us
  transfers between devices with their start and end apart: 3 -> 0, of which waited for: 3 -> 0; matrix products, arithmetic and copies ran while one was open for 0% -> 0% of each run, Pallas kernels for 0% -> 0%
where the time goes in v1:
time: 99.8 us; the launch traced here: 99.1 us
  Pallas kernels  92 us (92%)
  local copies, waits for them, and re-layouts  6.38 us (6%)
    pallas_call x1, Pallas kernels, on_device(): pl.pallas_call(kernel, out_shape=(jax.ShapeDtypeStruct((2, 16, 32, 128),...  92 us
    unnamed x3, local copies, waits for them, and re-layouts  5.09 us

profile of v1, /device:TPU:1, one launch (start us, length us, event | category | flops | bytes accessed | tf_op | source)
XLA Modules:
  0.0 99.1 jit_solution(7468821798299103855)
XLA Ops:
  0.6 1.3 %reshape.22.target_ref = s32[8,256]{1,0:T(8,128)} reshape(s32[2048]{0:T(1024)} %param.12) | data formatting | bytes 16384 | tf_op jit(solution)/shard_map/reshape | solution.py:453
  1.9 2.0 %copy.10.map_ref = f32[16,25,256]{2,1,0:T(8,128)} copy(f32[16,25,256]{2,0,1:T(8,128)} %param.10) | data formatting | bytes 819200 | tf_op args[2]
  4.0 92.0 %adjoint.1 = (f32[2,16,32,128]{3,2,1,0:T(8,128)}, f32[1,128]{1,0:T(1,128)}) custom-call(s32[8]{0:T(128)} %live_ref.1, s32[8,256]{1,0:T(8,128)} %reshape.22.target_ref, s32[1,256]{1,0:T(1,128)} %bitcast.8, f32[1,512]{1,0:T(1,128)} %bitcast.7, f32[2,2048,1024]{2,1,0:T(8,128)} %bem_ref.1, f32[2,25,32,256]{3,2,1,0:T(8,128)} %disp_ref.1, ...), custom_call_target="tpu_custom_call" | custom-call | flops 25999998976 | bytes 20000000 | tf_op jit(solution)/shard_map/adjoint/pallas_call | solution.py:405
  96.0 1.9 %copy.13 = f32[2,512,128]{2,1,0:T(8,128)} copy(f32[2,512,128]{2,1,0:T(8,128)} %bitcast.5) | data formatting | bytes 1048576
  97.9 1.2 %copy.14 = f32[128]{0:T(128)} copy(f32[128]{0:T(128)} %bitcast.9) | data formatting | bytes 1024

commit v2 on v1

v2 whole, which is shorter than its diff:
```python
import functools

import jax
import jax.numpy as jnp
from jax import lax
from jax.experimental import pallas as pl
from jax.experimental.pallas import tpu as pltpu
from jax.sharding import PartitionSpec as P

MESH = pl.DeviceIdType.MESH
F32 = jnp.float32
BF16 = jnp.bfloat16

CHUNKS = 4
UNITS = ((0, 0, 2048), (1, 0, 2048), (2, 0, 2048), (3, 0, 2048))
GROUPS = ((0, 0, 2048), (1, 0, 2048), (2, 0, 2048), (3, 0, 2048))
OPENING = (
    ("T", 1), ("T", 2), ("X", 1), ("B", 0), ("P", 0), ("V", 0, 0), ("B", 1), ("X", 2), ("P", 1),
    ("V", 0, 1), ("T", 3), ("V", 1, 0), ("X", 3), ("P", 2), ("B", 2), ("B", 3), ("V", 2, 0),
    ("V", 1, 1), ("B", 4), ("P", 3), ("V", 3, 0), ("B", 5), ("B", 6), ("V", 0, 2), ("V", 2, 1),
    ("B", 7), ("V", 4, 0),
)
EVENTS = {
    (0, 1): (("V", 1, 2),),
    (0, 2): (("V", 3, 1),),
    (1, 0): (("V", 2, 2), ("V", 0, 3), ("V", 4, 1),),
    (1, 2): (("V", 3, 2),),
    (1, 3): (("V", 1, 3),),
    (2, 0): (("V", 4, 2),),
    (2, 1): (("V", 2, 3),),
    (2, 3): (("V", 3, 3),),
    (3, 0): (("V", 4, 3),),
}
FORWARD = (2, 4, 6, 7)
SEM = (0, 2, 4, 5, 7, 8, 10, 11)

def nt(a, b):
    return lax.dot_general(a, b, (((1,), (1,)), ((), ())), preferred_element_type=F32)


def nn(a, b):
    return jnp.dot(a, b, preferred_element_type=F32)


def halves(value):
    high = value.astype(BF16)
    return high, (value - high.astype(F32)).astype(BF16)


def one_hot(condition):
    return jnp.where(condition, 1.0, 0.0).astype(BF16)


def kernel(
    live_ref, target_ref, dof_ref, weight_ref, bem_ref, disp_ref, map_ref, fwd_ref,
    field_ref, grad_ref,
    disp, fmap, fwd, stage, pick, spread, trac, comp, got, rhs, rhs_hi, rhs_lo, bem_hi, bem_lo,
    mine, theirs, joined, partial, grad,
    in_sem, bem_sem, swap_s, swap_r, ag_s, ag_r, pair_s, pair_r, sum_s, sum_r,
):
    row = lax.axis_index("row")
    col = lax.axis_index("col")
    x, core = row // 2, row % 2
    z, y = col // 4, col % 4

    barrier = pltpu.get_barrier_semaphore()
    for d in range(1, 8):
        pl.semaphore_signal(barrier, inc=1, device_id=((row + d) % 8, col), device_id_type=MESH)
    for d in (1, 3):
        near = ((z + d) % 4) * 4 + y
        pl.semaphore_signal(barrier, inc=1, device_id=(row, near), device_id_type=MESH)
        near = z * 4 + (y + d) % 4
        pl.semaphore_signal(barrier, inc=1, device_id=(row, near), device_id_type=MESH)

    loads = [
        pltpu.make_async_copy(map_ref, fmap, in_sem.at[0]),
        pltpu.make_async_copy(disp_ref, disp, in_sem.at[1]),
        pltpu.make_async_copy(fwd_ref, fwd, in_sem.at[2]),
    ]

    def bem_load(i):
        rows = pl.ds(pl.multiple_of(i * 256, 256), 256)
        return pltpu.make_async_copy(
            bem_ref.at[:, rows, :], stage.at[i % 2], bem_sem.at[i % 2]
        )

    loads[0].start()
    loads[1].start()
    bem_load(0).start()
    bem_load(1).start()
    loads[2].start()

    lane = lax.broadcasted_iota(jnp.int32, (8, 256), 1)
    line = lax.broadcasted_iota(jnp.int32, (8, 256), 0)
    count = jnp.zeros((8, 256), jnp.int32)
    for o in range(8):
        count = jnp.where(line == o, live_ref[o], count)
    live = lane < count
    target = jnp.concatenate([target_ref[:, o * 256 : o * 256 + 256] for o in range(8)], axis=0)
    block = target >> 7
    within = target & 127
    members = jnp.concatenate(
        [jnp.where(live & (block == b), 1.0, 0.0) for b in range(8)], axis=0
    )
    before = lax.broadcasted_iota(jnp.int32, (256, 256), 0) < lax.broadcasted_iota(
        jnp.int32, (256, 256), 1
    )
    ranks = members * nn(members.astype(BF16), one_hot(before))
    rank = ranks[0:8]
    for b in range(1, 8):
        rank = rank + ranks[b * 8 : b * 8 + 8]
    place = jnp.where(live, block * 32 + rank.astype(jnp.int32), -1)
    own = jnp.sum(jnp.where(line == row, place, 0), axis=0, keepdims=True)
    tall = lax.broadcasted_iota(jnp.int32, (256, 256), 0)
    pick[...] = one_hot(tall == own)
    grad[...] = jnp.zeros_like(grad)

    def build_spread():
        wide = lax.broadcasted_iota(jnp.int32, (128, 256), 0)
        here = jnp.where(live & (block == row), place - row * 32 + line * 32, -1)
        total = jnp.zeros((128, 256), F32)
        for o in range(8):
            total = total + nt(
                one_hot(wide == within[o : o + 1]), one_hot(tall == here[o : o + 1])
            )
        spread[...] = total.astype(BF16)

    def mask_map():
        loads[0].wait()
        node = lax.broadcasted_iota(jnp.int32, (25, 16, 256), 0)
        used = node < dof_ref[...].reshape(1, 1, 256)
        fmap[...] = jnp.where(used, fmap[...], 0.0)
        loads[1].wait()

    def swap(j, d):
        to = (row + d) % 8
        return pltpu.make_async_remote_copy(
            comp.at[j, pl.ds(pl.multiple_of(to * 32, 32), 32), :],
            got.at[j, pl.ds(pl.multiple_of(row * 32, 32), 32), :],
            swap_s.at[j, d - 1], swap_r.at[j, d - 1],
            device_id=(to, col), device_id_type=MESH,
        )

    def swap_in(j, d):
        origin = (row + 8 - d) % 8
        return pltpu.make_async_remote_copy(
            comp.at[j, pl.ds(pl.multiple_of(row * 32, 32), 32), :],
            got.at[j, pl.ds(pl.multiple_of(origin * 32, 32), 32), :],
            swap_s.at[j, d - 1], swap_r.at[j, d - 1],
            device_id=((row + d) % 8, col), device_id_type=MESH,
        )

    def tractions(j):
        eight = pl.ds(j * 8, 8)
        for group in range(4):
            sums = [[None] * 4, [None] * 4]
            for q in range(25):
                value = [disp[l, q, eight, :] for l in range(2)]
                for k in range(4):
                    at = group * 4 + k
                    scale = fmap[q, at : at + 1, :]
                    for l in range(2):
                        term = scale * value[l]
                        sums[l][k] = term if q == 0 else sums[l][k] + term
            for l in range(2):
                for k in range(4):
                    at = l * 128 + (group * 4 + k) * 8
                    trac[at : at + 8, :] = sums[l][k]
        high, low = halves(trac[...])
        comp[j] = nt(pick[...], high) + nt(pick[...], low)

    def exchange(j):
        for d in range(1, 8):
            swap(j, d).start()
        rows = pl.ds(pl.multiple_of(row * 32, 32), 32)
        got[j, rows, :] = comp[j, rows, :]

    def slots(f, first, second):
        def sel(v):
            kind, a = v
            return (a // 2, a % 2) if kind == "one" else (slice(None), a)

        fi, se = sel(first), sel(second)
        return fi + se if f == 0 else se + fi

    def part(ref, u, f, first, second):
        j, lane0, size = UNITS[u]
        return ref.at[(j,) + slots(f, first, second) + (f, slice(None), pl.ds(lane0, size))]

    def ring(f):
        return (z, y) if f == 0 else (y, z)

    def away(f, axis, step):
        v1, v2 = ring(f)
        if axis == 0:
            v1 = (v1 + step + 4) % 4
        else:
            v2 = (v2 + step + 4) % 4
        return (row, v1 * 4 + v2) if f == 0 else (row, v2 * 4 + v1)

    turn = 1 - 2 * core

    def hop(u, f, kind, step):
        v1, v2 = ring(f)
        back = lambda v, n: (v + 4 - n * step) % 4
        one = lambda v: ("one", v)
        par = ("par", (v1 + 1) % 2)
        far = one((v1 + 2) % 4)
        axis, out, into = {
            0: (0, (one(v1), one(v2)), (one(back(v1, 1)), one(v2))),
            1: (1, (one(v1), one(v2)), (one(v1), one(back(v2, 1)))),
            2: (0, (one(back(v1, 1)), one(v2)), (far, one(v2))),
            3: (1, (par, one(v2)), (par, one(back(v2, 1)))),
            4: (1, (one(v1), one(back(v2, 1))), (one(v1), one((v2 + 2) % 4))),
            5: (1, (far, one(v2)), (far, one(back(v2, 1)))),
            6: (1, (par, one(back(v2, 1))), (par, one((v2 + 2) % 4))),
            7: (1, (far, one(back(v2, 1))), (far, one((v2 + 2) % 4))),
        }[kind]
        n = SEM[kind] + (0 if kind in FORWARD or step == 1 else 1)
        make = lambda src, dst: pltpu.make_async_remote_copy(
            part(rhs, u, f, *src), part(rhs, u, f, *dst),
            ag_s.at[u, f, n], ag_r.at[u, f, n],
            device_id=away(f, axis, step), device_id_type=MESH,
        )
        return lambda: make(out, out), lambda: make(out, into)

    def steps(kind):
        return (turn,) if kind in FORWARD else (1, -1)

    def begin(u, kinds):
        for kind in kinds:
            for f in range(2):
                for step in steps(kind):
                    hop(u, f, kind, step)[0]().start()

    def arrive(u, kinds):
        for kind in kinds:
            for f in range(2):
                for step in steps(kind):
                    hop(u, f, kind, step)[1]().wait_recv()

    def gather_stage(u, which):
        if which == 0:
            begin(u, (0, 1))
        elif which == 1:
            arrive(u, (0,))
            begin(u, (2, 3))
            arrive(u, (1,))
            begin(u, (4,))
        elif which == 2:
            arrive(u, (2,))
            begin(u, (5,))
            arrive(u, (3,))
            begin(u, (6,))
        elif which == 3:
            arrive(u, (5,))
            begin(u, (7,))
        else:
            arrive(u, (4, 6, 7))

    def position(j):
        for d in range(1, 8):
            swap_in(j, d).wait_recv()
        high, low = halves(got[j])
        placed = nn(spread[...], high) + nn(spread[...], low)
        placed = placed.T
        for l in range(2):
            for p in range(16):
                at = l * 128 + p * 8
                rhs[j, z // 2, z % 2, y // 2, y % 2, l, :, p * 128 : p * 128 + 128] = placed[
                    at : at + 8, :
                ]

    def split_bem(i):
        bem_load(i).wait()

        @pl.loop(0, 16)
        def _(k):
            src = pl.ds(pl.multiple_of(k * 16, 16), 16)
            dst = pl.ds(pl.multiple_of(i * 256 + k * 16, 16), 16)
            real, imag = stage[i % 2, 0, src, :], stage[i % 2, 1, src, :]
            for m, value in enumerate((real, imag - real, real + imag)):
                high, low = halves(value)
                bem_hi[m, dst, :] = high
                bem_lo[m, dst, :] = low

        if i + 2 < 8:
            bem_load(i + 2).start()

    def split_rhs(j, lane0, size):
        lanes = pl.ds(lane0, size)
        for c in range(0, 16, 2):
            at = (j, c // 8, (c // 4) % 2, (c // 2) % 2)
            real = rhs[at + (slice(None), 0, slice(None), lanes)].reshape(16, size)
            imag = rhs[at + (slice(None), 1, slice(None), lanes)].reshape(16, size)
            for m, value in enumerate((real + imag, real, imag)):
                high, low = halves(value)
                rhs_hi[m, c * 8 : c * 8 + 16, lanes] = high
                rhs_lo[m, c * 8 : c * 8 + 16, lanes] = low

    def pair(j, t):
        return pltpu.make_async_remote_copy(
            theirs.at[j, t], joined.at[j, t], pair_s.at[j, t], pair_r.at[j, t],
            device_id=(x * 2 + 1 - core, col), device_id_type=MESH,
        )

    def share(j, t):
        return pltpu.make_async_remote_copy(
            mine.at[j, t], partial.at[j, t], sum_s.at[j, t], sum_r.at[j, t],
            device_id=(((x + 1 + t) % 4) * 2 + core, col), device_id_type=MESH,
        )

    def multiply(j, lane0, size, t):
        cols = pl.ds(pl.multiple_of(((x + 1 + t) % 4) * 256, 256), 256)
        part = pl.ds(lane0, size)
        both, cross, twin = [
            nn(rhs_hi[m, :, part], bem_hi[m, part, cols])
            + nn(rhs_hi[m, :, part], bem_lo[m, part, cols])
            + nn(rhs_lo[m, :, part], bem_hi[m, part, cols])
            for m in range(3)
        ]
        for l, value in enumerate((both - twin, both + cross)):
            left, right = value[:, :128], value[:, 128:]
            first = jnp.where(core == 0, left, right)
            second = jnp.where(core == 0, right, left)
            if lane0 > 0:
                first = mine[j, t, l] + first
                second = theirs[j, t, l] + second
            mine[j, t, l] = first
            theirs[j, t, l] = second
        if lane0 + size == 2048:
            pair(j, t).start()

    def share_if(j, t):
        if isinstance(t, int):
            if t < 3:
                share(j, t).start()
        else:

            @pl.when(t < 3)
            def _():
                share(j, t).start()

    def pass_on(j, t):
        pair(j, t).wait_recv()
        mine[j, t] = mine[j, t] + joined[j, t]

        share_if(j, t)

    def finish(j):
        for t in range(3):
            share(j, t).wait_recv()
        eight = pl.ds(j * 8, 8)
        for l in range(2):
            value = mine[j, 3, l] + partial[j, 0, l] + partial[j, 1, l] + partial[j, 2, l]
            value = value.reshape(16, 8, 128)
            field_ref[l, :, eight, :] = value
            grad[...] += jnp.sum(fwd[l, :, eight, :] * value, axis=0)

    def weigh():
        loads[2].wait()
        weight = jnp.broadcast_to(weight_ref[...], (128, 512)).T.reshape(16, 32, 128)
        for l in range(2):
            fwd[l] = fwd[l] * weight

    def act(op):
        what = op[0]
        if what == "V":
            gather_stage(op[2], op[1])
        elif what == "T":
            tractions(op[1])
        elif what == "X":
            exchange(op[1])
        elif what == "P":
            position(op[1])
        else:
            split_bem(op[1])

    mask_map()
    tractions(0)
    pl.semaphore_wait(barrier, 11)
    exchange(0)
    build_spread()
    for op in OPENING:
        act(op)
    weigh()

    before = None
    for g, (j, lane0, size) in enumerate(GROUPS):
        last = lane0 + size == 2048
        for op in EVENTS.get((g, 0), ()):
            act(op)
        split_rhs(j, lane0, size)

        @pl.loop(0, 4)
        def _(t):
            for k in (1, 2, 3):
                if (g, k) in EVENTS:

                    @pl.when(t == k)
                    def _():
                        for op in EVENTS[(g, k)]:
                            act(op)

            multiply(j, lane0, size, t)
            if last:

                @pl.when(t >= 1)
                def _():
                    pass_on(j, t - 1)

            if before is not None:

                @pl.when(t == 0)
                def _():
                    pass_on(before, 3)

                @pl.when(t == 2)
                def _():
                    finish(before)

        before = j if last else None

    pass_on(CHUNKS - 1, 3)
    finish(CHUNKS - 1)
    grad_ref[...] = jnp.sum(grad[...], axis=0, keepdims=True)

    for u in range(len(UNITS)):
        for f in range(2):
            for kind in range(8):
                for step in steps(kind):
                    hop(u, f, kind, step)[0]().wait_send()
    for j in range(CHUNKS):
        for d in range(1, 8):
            swap(j, d).wait_send()
        for t in range(4):
            pair(j, t).wait_send()
        for t in range(3):
            share(j, t).wait_send()


def on_device(
    bem, face_disp, face_map, dof_count, elem_target, live_count, forward_field, power_weight
):
    vmem = pl.BlockSpec(memory_space=pltpu.VMEM)
    hbm = pl.BlockSpec(memory_space=pl.ANY)
    dma = pltpu.SemaphoreType.DMA
    field, gradient = pl.pallas_call(
        kernel,
        out_shape=(
            jax.ShapeDtypeStruct((2, 16, 32, 128), F32),
            jax.ShapeDtypeStruct((1, 128), F32),
        ),
        in_specs=[pl.BlockSpec(memory_space=pltpu.SMEM), vmem, vmem, vmem, hbm, hbm, hbm, hbm],
        out_specs=(vmem, vmem),
        scratch_shapes=[
            pltpu.VMEM((2, 25, 32, 256), F32),
            pltpu.VMEM((25, 16, 256), F32),
            pltpu.VMEM((2, 16, 32, 128), F32),
            pltpu.VMEM((2, 2, 256, 1024), F32),
            pltpu.VMEM((256, 256), BF16),
            pltpu.VMEM((128, 256), BF16),
            pltpu.VMEM((256, 256), F32),
            pltpu.VMEM((CHUNKS, 256, 256), F32),
            pltpu.VMEM((CHUNKS, 256, 256), F32),
            pltpu.VMEM((CHUNKS, 2, 2, 2, 2, 2, 8, 2048), F32),
            pltpu.VMEM((3, 128, 2048), BF16),
            pltpu.VMEM((3, 128, 2048), BF16),
            pltpu.VMEM((3, 2048, 1024), BF16),
            pltpu.VMEM((3, 2048, 1024), BF16),
            pltpu.VMEM((CHUNKS, 4, 2, 128, 128), F32),
            pltpu.VMEM((CHUNKS, 4, 2, 128, 128), F32),
            pltpu.VMEM((CHUNKS, 4, 2, 128, 128), F32),
            pltpu.VMEM((CHUNKS, 3, 2, 128, 128), F32),
            pltpu.VMEM((8, 128), F32),
            dma((3,)),
            dma((2,)),
            dma((CHUNKS, 7)),
            dma((CHUNKS, 7)),
            dma((len(UNITS), 2, 12)),
            dma((len(UNITS), 2, 12)),
            dma((CHUNKS, 4)),
            dma((CHUNKS, 4)),
            dma((CHUNKS, 3)),
            dma((CHUNKS, 3)),
        ],
        compiler_params=pltpu.CompilerParams(
            collective_id=0, has_side_effects=True, vmem_limit_bytes=60 * 2**20
        ),
        cost_estimate=pl.CostEstimate(
            flops=26 * 10**9, bytes_accessed=20 * 10**6, transcendentals=0
        ),
        name="adjoint",
    )(
        live_count,
        elem_target.reshape(1, 2048),
        dof_count.reshape(1, 256),
        power_weight.reshape(1, 512),
        bem,
        face_disp,
        jnp.transpose(face_map, (1, 0, 2)),
        forward_field.reshape(2, 16, 32, 128),
    )
    return field.reshape(2, 512, 128), gradient.reshape(128)


def solution(mesh):
    placed = (
        P(None, "row", "col"),
        P(None, None, "col", "row"),
        P(None, None, "row"),
        P("row"),
        P(),
        P(),
        P(None, None, ("col", "row")),
        P(),
    )
    return jax.shard_map(
        on_device,
        mesh=mesh,
        in_specs=placed,
        out_specs=(P(None, None, ("col", "row")), P(("col", "row"))),
        check_vma=False,
    )
```

time: 99.8 us -> 83.3 us (0.83)
  Pallas kernels: 92 us -> 79.4 us
  local copies, waits for them, and re-layouts: 6.38 us -> 2.97 us
    pallas_call x1, Pallas kernels: 92 us -> 79.4 us  [on_device(): pl.pallas_call(kernel, out_shape=(jax.ShapeDtypeStruct((2, 16, 32, 128),...]
    unnamed x3 -> x2, local copies, waits for them, and re-layouts: 5.09 us -> 2.97 us
    reshape x1 -> x0, local copies, waits for them, and re-layouts: 1.29 us -> none  [on_device(): elem_target.reshape(8, 256)]
where the time goes in v2:
time: 83.3 us; the launch traced here: 83 us
  Pallas kernels  79.4 us (95%)
  local copies, waits for them, and re-layouts  2.97 us (4%)
    pallas_call x1, Pallas kernels, on_device(): pl.pallas_call(kernel, out_shape=(jax.ShapeDtypeStruct((2, 16, 32, 128),...  79.4 us
    unnamed x2, local copies, waits for them, and re-layouts  2.97 us

profile of v2, /device:TPU:1, one launch (start us, length us, event | category | flops | bytes accessed | tf_op | source)
XLA Modules:
  0.0 83.0 jit_solution(2240884564395937722)
XLA Ops:
  0.6 79.4 %adjoint.1 = (f32[2,16,32,128]{3,2,1,0:T(8,128)}, f32[1,128]{1,0:T(1,128)}) custom-call(s32[8]{0:T(128)} %live_ref.1, s32[1,2048]{1,0:T(1,128)} %bitcast.10, s32[1,256]{1,0:T(1,128)} %bitcast.12, f32[1,512]{1,0:T(1,128)} %bitcast.11, f32[2,2048,1024]{2,1,0:T(8,128)} %bem_ref.1, f32[2,25,32,256]{3,2,1,0:T(8,128)} %disp_ref.1, f32[25,16,256]{2,1,0:T(8,128)} %bitcast.9, ...), custom_call_target="tpu_custom_call" | custom-call | flops 25999998976 | bytes 20000000 | tf_op jit(solution)/shard_map/adjoint/pallas_call | solution.py:448
  80.1 1.9 %copy.12 = f32[2,512,128]{2,1,0:T(8,128)} copy(f32[2,512,128]{2,1,0:T(8,128)} %bitcast.7) | data formatting | bytes 1048576
  81.9 1.1 %copy.13 = f32[128]{0:T(128)} copy(f32[128]{0:T(128)} %bitcast.13) | data formatting | bytes 1024

commit v3 on v2

--- a/solution.py
+++ b/solution.py
@@ -12,24 +12,80 @@
 BF16 = jnp.bfloat16
 
 CHUNKS = 4
-UNITS = ((0, 0, 2048), (1, 0, 2048), (2, 0, 2048), (3, 0, 2048))
-GROUPS = ((0, 0, 2048), (1, 0, 2048), (2, 0, 2048), (3, 0, 2048))
+UNITS = tuple((j, 0, 2048) for j in range(CHUNKS))
+GROUPS = ((0, 0, 4), (1, 0, 4), (2, 0, 3), (3, 0, 4), (2, 3, 4))
 OPENING = (
-    ("T", 1), ("T", 2), ("X", 1), ("B", 0), ("P", 0), ("V", 0, 0), ("B", 1), ("X", 2), ("P", 1),
-    ("V", 0, 1), ("T", 3), ("V", 1, 0), ("X", 3), ("P", 2), ("B", 2), ("B", 3), ("V", 2, 0),
-    ("V", 1, 1), ("B", 4), ("P", 3), ("V", 3, 0), ("B", 5), ("B", 6), ("V", 0, 2), ("V", 2, 1),
-    ("B", 7), ("V", 4, 0),
+    ("B", 0), ("B", 1), ("T", 1), ("X", 1), ("B", 2), ("P", 0), ("V", 0, 0), ("B", 3), ("P", 1),
+    ("V", 0, 1), ("T", 2), ("V", 1, 0), ("T", 3), ("X", 2), ("X", 3), ("V", 2, 0), ("B", 4),
+    ("V", 1, 1), ("P", 2), ("V", 3, 0), ("P", 3), ("B", 5), ("B", 6), ("V", 0, 2), ("B", 7),
+    ("V", 4, 0), ("V", 2, 1),
 )
 EVENTS = {
-    (0, 1): (("V", 1, 2),),
-    (0, 2): (("V", 3, 1),),
-    (1, 0): (("V", 2, 2), ("V", 0, 3), ("V", 4, 1),),
-    (1, 2): (("V", 3, 2),),
-    (1, 3): (("V", 1, 3),),
-    (2, 0): (("V", 4, 2),),
-    (2, 1): (("V", 2, 3),),
-    (2, 3): (("V", 3, 3),),
-    (3, 0): (("V", 4, 3),),
+    (0, 1): (
+        ("V", 1, 2),
+    ),
+    (0, 2): (
+        ("V", 3, 1), ("R", 0, 0),
+    ),
+    (0, 3): (
+        ("V", 0, 3),
+    ),
+    (1, 0): (
+        ("V", 2, 2), ("V", 4, 1),
+    ),
+    (1, 1): (
+        ("V", 1, 3),
+    ),
+    (1, 3): (
+        ("V", 3, 2), ("R", 1, 1), ("F", 0),
+    ),
+    (2, 0): (
+        ("V", 2, 3), ("V", 4, 2),
+    ),
+    (2, 2): (
+        ("V", 3, 3), ("R", 2, 0),
+    ),
+    (3, 0): (
+        ("V", 4, 3),
+    ),
+    (3, 3): (
+        ("R", 3, 2),
+    ),
+}
+AFTER = {
+    (0, 2): (
+        ("R", 0, 1),
+    ),
+    (0, 3): (
+        ("R", 0, 2),
+    ),
+    (1, 0): (
+        ("R", 0, 3),
+    ),
+    (1, 1): (
+        ("R", 1, 0),
+    ),
+    (1, 3): (
+        ("R", 1, 2),
+    ),
+    (2, 0): (
+        ("R", 1, 3),
+    ),
+    (2, 2): (
+        ("R", 2, 1), ("F", 1),
+    ),
+    (3, 0): (
+        ("R", 2, 2),
+    ),
+    (3, 1): (
+        ("R", 3, 0),
+    ),
+    (3, 2): (
+        ("R", 3, 1),
+    ),
+    (4, 3): (
+        ("R", 3, 3), ("R", 2, 3), ("F", 2), ("F", 3),
+    ),
 }
 FORWARD = (2, 4, 6, 7)
 SEM = (0, 2, 4, 5, 7, 8, 10, 11)
@@ -170,7 +226,7 @@
         comp[j] = nt(pick[...], high) + nt(pick[...], low)
 
     def exchange(j):
-        for d in range(1, 8):
+        for d in (4, 5, 2, 3, 6, 7, 1):
             swap(j, d).start()
         rows = pl.ds(pl.multiple_of(row * 32, 32), 32)
         got[j, rows, :] = comp[j, rows, :]
@@ -271,6 +327,9 @@
                     at : at + 8, :
                 ]
 
+    def chip(t):
+        return (x + 2 + 3 * t - t * (t - 1) // 2) % 4
+
     def split_bem(i):
         bem_load(i).wait()
 
@@ -278,25 +337,26 @@
         def _(k):
             src = pl.ds(pl.multiple_of(k * 16, 16), 16)
             dst = pl.ds(pl.multiple_of(i * 256 + k * 16, 16), 16)
-            real, imag = stage[i % 2, 0, src, :], stage[i % 2, 1, src, :]
-            for m, value in enumerate((real, imag - real, real + imag)):
-                high, low = halves(value)
-                bem_hi[m, dst, :] = high
-                bem_lo[m, dst, :] = low
+            for t in range(4):
+                cols = pl.ds(pl.multiple_of(chip(t) * 256, 256), 256)
+                real, imag = stage[i % 2, 0, src, cols], stage[i % 2, 1, src, cols]
+                for m, value in enumerate((real, imag - real, real + imag)):
+                    high, low = halves(value)
+                    bem_hi[m, dst, t * 256 : t * 256 + 256] = high
+                    bem_lo[m, dst, t * 256 : t * 256 + 256] = low
 
         if i + 2 < 8:
             bem_load(i + 2).start()
 
-    def split_rhs(j, lane0, size):
-        lanes = pl.ds(lane0, size)
+    def split_rhs(j):
         for c in range(0, 16, 2):
             at = (j, c // 8, (c // 4) % 2, (c // 2) % 2)
-            real = rhs[at + (slice(None), 0, slice(None), lanes)].reshape(16, size)
-            imag = rhs[at + (slice(None), 1, slice(None), lanes)].reshape(16, size)
+            real = rhs[at + (slice(None), 0)].reshape(16, 2048)
+            imag = rhs[at + (slice(None), 1)].reshape(16, 2048)
             for m, value in enumerate((real + imag, real, imag)):
                 high, low = halves(value)
-                rhs_hi[m, c * 8 : c * 8 + 16, lanes] = high
-                rhs_lo[m, c * 8 : c * 8 + 16, lanes] = low
+                rhs_hi[m, c * 8 : c * 8 + 16, :] = high
+                rhs_lo[m, c * 8 : c * 8 + 16, :] = low
 
     def pair(j, t):
         return pltpu.make_async_remote_copy(
@@ -307,45 +367,29 @@
     def share(j, t):
         return pltpu.make_async_remote_copy(
             mine.at[j, t], partial.at[j, t], sum_s.at[j, t], sum_r.at[j, t],
-            device_id=(((x + 1 + t) % 4) * 2 + core, col), device_id_type=MESH,
+            device_id=(chip(t) * 2 + core, col), device_id_type=MESH,
         )
 
-    def multiply(j, lane0, size, t):
-        cols = pl.ds(pl.multiple_of(((x + 1 + t) % 4) * 256, 256), 256)
-        part = pl.ds(lane0, size)
+    def multiply(j, t):
+        cols = pl.ds(pl.multiple_of(t * 256, 256), 256)
         both, cross, twin = [
-            nn(rhs_hi[m, :, part], bem_hi[m, part, cols])
-            + nn(rhs_hi[m, :, part], bem_lo[m, part, cols])
-            + nn(rhs_lo[m, :, part], bem_hi[m, part, cols])
+            nn(rhs_hi[m], bem_hi[m, :, cols])
+            + nn(rhs_hi[m], bem_lo[m, :, cols])
+            + nn(rhs_lo[m], bem_hi[m, :, cols])
             for m in range(3)
         ]
         for l, value in enumerate((both - twin, both + cross)):
             left, right = value[:, :128], value[:, 128:]
-            first = jnp.where(core == 0, left, right)
-            second = jnp.where(core == 0, right, left)
-            if lane0 > 0:
-                first = mine[j, t, l] + first
-                second = theirs[j, t, l] + second
-            mine[j, t, l] = first
-            theirs[j, t, l] = second
-        if lane0 + size == 2048:
-            pair(j, t).start()
-
-    def share_if(j, t):
-        if isinstance(t, int):
-            if t < 3:
-                share(j, t).start()
-        else:
-
-            @pl.when(t < 3)
-            def _():
-                share(j, t).start()
+            mine[j, t, l] = jnp.where(core == 0, left, right)
+            theirs[j, t, l] = jnp.where(core == 0, right, left)
+        pair(j, t).start()
 
     def pass_on(j, t):
         pair(j, t).wait_recv()
         mine[j, t] = mine[j, t] + joined[j, t]
 
-        share_if(j, t)
+        if t < 3:
+            share(j, t).start()
 
     def finish(j):
         for t in range(3):
@@ -371,6 +415,10 @@
             tractions(op[1])
         elif what == "X":
             exchange(op[1])
+        elif what == "R":
+            pass_on(op[1], op[2])
+        elif what == "F":
+            finish(op[1])
         elif what == "P":
             position(op[1])
         else:
@@ -385,16 +433,14 @@
         act(op)
     weigh()
 
-    before = None
-    for g, (j, lane0, size) in enumerate(GROUPS):
-        last = lane0 + size == 2048
-        for op in EVENTS.get((g, 0), ()):
+    for g, (j, low, high) in enumerate(GROUPS):
+        for op in EVENTS.get((g, low), ()):
             act(op)
-        split_rhs(j, lane0, size)
-
-        @pl.loop(0, 4)
+        split_rhs(j)
+
+        @pl.loop(low, high)
         def _(t):
-            for k in (1, 2, 3):
+            for k in range(low + 1, high):
                 if (g, k) in EVENTS:
 
                     @pl.when(t == k)
@@ -402,27 +448,15 @@
                         for op in EVENTS[(g, k)]:
                             act(op)
 
-            multiply(j, lane0, size, t)
-            if last:
-
-                @pl.when(t >= 1)
-                def _():
-                    pass_on(j, t - 1)
-
-            if before is not None:
-
-                @pl.when(t == 0)
-                def _():
-                    pass_on(before, 3)
-
-                @pl.when(t == 2)
-                def _():
-                    finish(before)
-
-        before = j if last else None
-
-    pass_on(CHUNKS - 1, 3)
-    finish(CHUNKS - 1)
+            multiply(j, t)
+            for k in range(low, high):
+                if (g, k) in AFTER:
+
+                    @pl.when(t == k)
+                    def _():
+                        for op in AFTER[(g, k)]:
+                            act(op)
+
     grad_ref[...] = jnp.sum(grad[...], axis=0, keepdims=True)
 
     for u in range(len(UNITS)):
@@ -447,10 +481,7 @@
     dma = pltpu.SemaphoreType.DMA
     field, gradient = pl.pallas_call(
         kernel,
-        out_shape=(
-            jax.ShapeDtypeStruct((2, 16, 32, 128), F32),
-            jax.ShapeDtypeStruct((1, 128), F32),
-        ),
+        out_shape=(pltpu.VMEM((2, 16, 32, 128), F32), pltpu.VMEM((1, 128), F32)),
         in_specs=[pl.BlockSpec(memory_space=pltpu.SMEM), vmem, vmem, vmem, hbm, hbm, hbm, hbm],
         out_specs=(vmem, vmem),
         scratch_shapes=[

time: 83.3 us -> 80.4 us (0.965)
  local copies, waits for them, and re-layouts: 2.97 us -> 1.31 us
  Pallas kernels: 79.4 us -> 78.3 us
    unnamed x2, local copies, waits for them, and re-layouts: 2.97 us -> 1.31 us
    pallas_call x1, Pallas kernels: 79.4 us -> 78.3 us  [on_device(): pl.pallas_call(kernel, out_shape=(pltpu.VMEM((2, 16, 32, 128), F32), pltp...]
where the time goes in v3:
time: 80.4 us; the launch traced here: 80.2 us
  Pallas kernels  78.3 us (97%)
  local copies, waits for them, and re-layouts  1.31 us (2%)
    pallas_call x1, Pallas kernels, on_device(): pl.pallas_call(kernel, out_shape=(pltpu.VMEM((2, 16, 32, 128), F32), pltp...  78.3 us

profile of v3, /device:TPU:1, one launch (start us, length us, event | category | flops | bytes accessed | tf_op | source)
XLA Modules:
  0.0 80.2 jit_solution(5692799457675055174)
XLA Ops:
  0.6 78.3 %adjoint.1 = (f32[2,16,32,128]{3,2,1,0:T(8,128)S(1)}, f32[1,128]{1,0:T(1,128)S(1)}) custom-call(s32[8]{0:T(128)} %live_ref.1, s32[1,2048]{1,0:T(1,128)} %bitcast.11, s32[1,256]{1,0:T(1,128)} %bitcast.13, f32[1,512]{1,0:T(1,128)} %bitcast.12, f32[2,2048,1024]{2,1,0:T(8,128)} %bem_ref.1, f32[2,25,32,256]{3,2,1,0:T(8,128)} %disp_ref.1, ...), custom_call_target="tpu_custom_call" | custom-call | flops 25999998976 | bytes 20000000 | tf_op jit(solution)/shard_map/adjoint/pallas_call | solution.py:482
  78.9 0.8 copy.12
  79.7 0.5 copy.13

commit v4 on v3

--- a/solution.py
+++ b/solution.py
@@ -15,10 +15,10 @@
 UNITS = tuple((j, 0, 2048) for j in range(CHUNKS))
 GROUPS = ((0, 0, 4), (1, 0, 4), (2, 0, 3), (3, 0, 4), (2, 3, 4))
 OPENING = (
-    ("B", 0), ("B", 1), ("T", 1), ("X", 1), ("B", 2), ("P", 0), ("V", 0, 0), ("B", 3), ("P", 1),
-    ("V", 0, 1), ("T", 2), ("V", 1, 0), ("T", 3), ("X", 2), ("X", 3), ("V", 2, 0), ("B", 4),
-    ("V", 1, 1), ("P", 2), ("V", 3, 0), ("P", 3), ("B", 5), ("B", 6), ("V", 0, 2), ("B", 7),
-    ("V", 4, 0), ("V", 2, 1),
+    ("T", 1), ("X", 1), ("P", 0), ("V", 0, 0), ("T", 2), ("X", 2), ("P", 1), ("V", 0, 1), ("B", 0),
+    ("V", 1, 0), ("B", 1), ("B", 2), ("T", 3), ("X", 3), ("G", 0), ("V", 2, 0), ("B", 3), ("V", 1, 1),
+    ("P", 2), ("B", 4), ("B", 5), ("V", 3, 0), ("V", 0, 2), ("B", 6), ("P", 3), ("V", 2, 1),
+    ("B", 7), ("V", 4, 0),
 )
 EVENTS = {
     (0, 1): (
@@ -28,51 +28,45 @@
         ("V", 3, 1), ("R", 0, 0),
     ),
     (0, 3): (
-        ("V", 0, 3),
+        ("V", 0, 3), ("R", 0, 1),
     ),
     (1, 0): (
-        ("V", 2, 2), ("V", 4, 1),
+        ("V", 2, 2), ("R", 0, 2), ("V", 4, 1),
     ),
     (1, 1): (
         ("V", 1, 3),
     ),
     (1, 3): (
-        ("V", 3, 2), ("R", 1, 1), ("F", 0),
+        ("V", 3, 2), ("F", 0),
     ),
     (2, 0): (
-        ("V", 2, 3), ("V", 4, 2),
-    ),
-    (2, 2): (
-        ("V", 3, 3), ("R", 2, 0),
+        ("V", 2, 3), ("R", 1, 2), ("V", 4, 2),
+    ),
+    (2, 1): (
+        ("V", 3, 3),
     ),
     (3, 0): (
-        ("V", 4, 3),
+        ("V", 4, 3), ("R", 2, 1), ("F", 1),
     ),
     (3, 3): (
         ("R", 3, 2),
     ),
 }
 AFTER = {
-    (0, 2): (
-        ("R", 0, 1),
-    ),
-    (0, 3): (
-        ("R", 0, 2),
-    ),
     (1, 0): (
         ("R", 0, 3),
     ),
     (1, 1): (
         ("R", 1, 0),
     ),
-    (1, 3): (
-        ("R", 1, 2),
+    (1, 2): (
+        ("R", 1, 1),
     ),
     (2, 0): (
         ("R", 1, 3),
     ),
-    (2, 2): (
-        ("R", 2, 1), ("F", 1),
+    (2, 1): (
+        ("R", 2, 0),
     ),
     (3, 0): (
         ("R", 2, 2),
@@ -84,6 +78,7 @@
         ("R", 3, 1),
     ),
     (4, 3): (
+        ("W", 0),
         ("R", 3, 3), ("R", 2, 3), ("F", 2), ("F", 3),
     ),
 }
@@ -407,6 +402,16 @@
         for l in range(2):
             fwd[l] = fwd[l] * weight
 
+    def drain():
+        for u in range(len(UNITS)):
+            for f in range(2):
+                for kind in range(8):
+                    for step in steps(kind):
+                        hop(u, f, kind, step)[0]().wait_send()
+        for j in range(CHUNKS):
+            for d in range(1, 8):
+                swap(j, d).wait_send()
+
     def act(op):
         what = op[0]
         if what == "V":
@@ -415,6 +420,10 @@
             tractions(op[1])
         elif what == "X":
             exchange(op[1])
+        elif what == "G":
+            weigh()
+        elif what == "W":
+            drain()
         elif what == "R":
             pass_on(op[1], op[2])
         elif what == "F":
@@ -431,7 +440,6 @@
     build_spread()
     for op in OPENING:
         act(op)
-    weigh()
 
     for g, (j, low, high) in enumerate(GROUPS):
         for op in EVENTS.get((g, low), ()):
@@ -459,14 +467,7 @@
 
     grad_ref[...] = jnp.sum(grad[...], axis=0, keepdims=True)
 
-    for u in range(len(UNITS)):
-        for f in range(2):
-            for kind in range(8):
-                for step in steps(kind):
-                    hop(u, f, kind, step)[0]().wait_send()
     for j in range(CHUNKS):
-        for d in range(1, 8):
-            swap(j, d).wait_send()
         for t in range(4):
             pair(j, t).wait_send()
         for t in range(3):

time: 80.4 us -> 79.8 us (level)
  no operation moved by 1% of the time
where the time goes in v4:
time: 79.8 us; the launch traced here: 79.6 us
  Pallas kernels  77.6 us (97%)
  local copies, waits for them, and re-layouts  1.31 us (2%)
    pallas_call x1, Pallas kernels, on_device(): pl.pallas_call(kernel, out_shape=(pltpu.VMEM((2, 16, 32, 128), F32), pltp...  77.6 us

profile of v4, /device:TPU:1, one launch (start us, length us, event | category | flops | bytes accessed | tf_op | source)
XLA Modules:
  0.0 79.6 jit_solution(8817230637559472732)
XLA Ops:
  0.6 77.6 %adjoint.1 = (f32[2,16,32,128]{3,2,1,0:T(8,128)S(1)}, f32[1,128]{1,0:T(1,128)S(1)}) custom-call(s32[8]{0:T(128)} %live_ref.1, s32[1,2048]{1,0:T(1,128)} %bitcast.11, s32[1,256]{1,0:T(1,128)} %bitcast.13, f32[1,512]{1,0:T(1,128)} %bitcast.12, f32[2,2048,1024]{2,1,0:T(8,128)} %bem_ref.1, f32[2,25,32,256]{3,2,1,0:T(8,128)} %disp_ref.1, ...), custom_call_target="tpu_custom_call" | custom-call | flops 25999998976 | bytes 20000000 | tf_op jit(solution)/shard_map/adjoint/pallas_call | solution.py:483
  78.3 0.8 %copy.12 = f32[2,512,128]{2,1,0:T(8,128)} copy(f32[2,512,128]{2,1,0:T(8,128)S(1)} %bitcast.7) | data formatting | bytes 1048576
  79.1 0.5 copy.13
